TPU v7x, 256 devices: a whole 4x4x8 slice. The times are simulated.
256 devices in a mesh: expert: 64 (over z, y, core), ctx: 4 (over x).
Axes of the slice: x: 4, y: 4, z: 8, core: 2. Of those that a mesh axis runs over, the one named last changes fastest.
Arguments:
- query: bfloat16 [128, 128, 576], P('expert'), may hold values from -72 to 72
- cache: bfloat16 [128, 8192, 576], P('expert', 'ctx'), may hold values from -6 to 6
- lengths: int32 [128], P('expert'), may hold values from 2048 to 8192
- blocks: int32 [128, 32], P('expert'), may hold values from 0 to 127, as said below
- moe_tokens: bfloat16 [1024, 7168], P('expert'), may hold values from -6 to 6
- routes: int32 [1024, 8], P('expert'), may hold values from 0 to 15, all different within a row; in each aligned block of 16 rows (0 to 15, 16 to 31, ...) at most 12 rows name the same one
- route_weights: float32 [1024, 8], P('expert'), may hold values from 0.05 to 0.6
- w_gate: bfloat16 [7168, 32768], P('ctx', 'expert'), may hold values from -0.0625 to 0.0625
- w_up: bfloat16 [7168, 32768], P('ctx', 'expert'), may hold values from -0.0625 to 0.0625
- w_down: bfloat16 [32768, 7168], P('expert', 'ctx'), may hold values from -0.125 to 0.125
Outputs:
- attn_out: bfloat16 [128, 128, 512], P('expert', 'ctx')
- moe_out: bfloat16 [1024, 7168], P('expert')
Inputs may be any that keep to these rules, and one draw needn't show every extreme that they name: A sequence's 32 block ids are distinct and ascending, each below the count of blocks that hold its tokens, and the last names the block of its newest token (position lengths - 1). `routes`: each row names 8 different experts; among the rows of one index of expert no expert is named by more than 12 rows, and in some index one is named by exactly 12.
All inputs are finite; a program needn't handle non-finite values.
Results may differ from a plain program's by a relative error of at most 0.0049.
Values may be sent and summed in bfloat16 or wider, within the bound.
A program may use at most 128 MiB of HBM per device.

v0:
```python
import jax
import jax.numpy as jnp
from jax import lax
from jax.sharding import PartitionSpec as P

FF = 2048
KV = 512
QK_DIM = 192
EXPERTS = 16
BLOCK = 64
CAP = 12


def joined(part, axis, combine):
    gathered = jax.tree.map(lambda a: lax.all_gather(a, axis), part)

    def take(source):
        return jax.tree.map(lambda a: lax.dynamic_index_in_dim(a, source, 0, False), gathered)

    return lax.fori_loop(
        1, lax.axis_size(axis), lambda source, state: combine(state, take(source)), take(0)
    )


def combine_partials(first_part, second_part):
    highest = jnp.maximum(first_part[0], second_part[0])
    left_factor = jnp.exp(first_part[0] - highest)
    right_factor = jnp.exp(second_part[0] - highest)
    return (
        highest,
        first_part[1] * left_factor + second_part[1] * right_factor,
        first_part[2] * left_factor[..., None] + second_part[2] * right_factor[..., None],
    )


def shards(query, cache, lengths, blocks, moe_tokens, routes, route_weights, w_gate, w_up, w_down):
    head_count = query.shape[1]
    token_span = cache.shape[1]
    ctx_count = lax.axis_size("ctx")
    ctx_index = lax.axis_index("ctx")
    positions = ctx_index * token_span + jnp.arange(token_span, dtype=jnp.int32)
    owning = positions // BLOCK
    chosen = jnp.any(blocks[:, :, None] == owning[None, None, :], axis=1)
    usable = chosen & (positions[None, :] < lengths[:, None])
    scores = jnp.einsum(
        "rhi,rti->rht", query, cache, preferred_element_type=jnp.float32
    ) * QK_DIM ** (-0.5)
    scores = jnp.where(usable[:, None, :], scores, -1e30)
    peak_score = jnp.max(scores, axis=2)
    weights = jnp.where(usable[:, None, :], jnp.exp(scores - peak_score[:, :, None]), 0.0)
    weight_sum = jnp.sum(weights, axis=2)
    latent_values = cache[:, :, :KV].astype(jnp.float32)
    weighted = jnp.einsum(
        "rht,rtc->rhc",
        weights,
        latent_values,
        precision=lax.Precision.HIGHEST,
        preferred_element_type=jnp.float32,
    )
    head_share = head_count // ctx_count
    merged = joined((peak_score, weight_sum, weighted), "ctx", combine_partials)
    head_start = ctx_index * head_share
    total_heads = lax.dynamic_slice_in_dim(merged[1], head_start, head_share, 1)
    weighted_heads = lax.dynamic_slice_in_dim(merged[2], head_start, head_share, 1)
    attn_out = (weighted_heads / total_heads[..., None]).astype(jnp.bfloat16)
    row_count = moe_tokens.shape[0]
    quarter = w_gate.shape[0]
    local_units = w_gate.shape[1]
    expert_count = lax.axis_size("expert")
    per_expert = max(1, local_units // FF)
    spread = max(1, FF // local_units)
    block_units = local_units // per_expert
    token_part = lax.dynamic_slice_in_dim(moe_tokens, ctx_index * quarter, quarter, 1)
    route_hits = routes[:, :, None] == jnp.arange(EXPERTS, dtype=jnp.int32)[None, None, :]
    expert_hits = jnp.sum(route_hits.astype(jnp.int32), axis=1)
    mixing = jnp.sum(jnp.where(route_hits, route_weights[:, :, None], 0.0), axis=1)
    slot_rank = jnp.cumsum(expert_hits, axis=0) - expert_hits
    slot_match = (expert_hits[:, :, None] == 1) & (
        slot_rank[:, :, None] == jnp.arange(CAP, dtype=jnp.int32)[None, None, :]
    )
    placing = slot_match.reshape(row_count, EXPERTS * CAP).astype(jnp.bfloat16)
    packed = jnp.dot(placing.T, token_part, preferred_element_type=jnp.float32).astype(jnp.bfloat16)
    packed = packed.reshape(EXPERTS // per_expert, 1, per_expert, CAP, quarter)
    outgoing = jnp.broadcast_to(
        packed, (EXPERTS // per_expert, spread, per_expert, CAP, quarter)
    ).reshape(expert_count, per_expert, CAP, quarter)
    gate_local = w_gate.reshape(quarter, per_expert, block_units)
    up_local = w_up.reshape(quarter, per_expert, block_units)
    down_local = w_down.reshape(per_expert, block_units, quarter)
    arrived = lax.all_to_all(outgoing, "expert", split_axis=0, concat_axis=0, tiled=True)
    gate_sum = jnp.einsum("sqnd,dqf->sqnf", arrived, gate_local, preferred_element_type=jnp.float32)
    up_sum = jnp.einsum("sqnd,dqf->sqnf", arrived, up_local, preferred_element_type=jnp.float32)
    gate_sum, up_sum = lax.psum((gate_sum, up_sum), "ctx")
    activated = (jax.nn.silu(gate_sum) * up_sum).astype(jnp.bfloat16)
    returned = lax.all_to_all(
        jnp.einsum("sqnf,qfd->sqnd", activated, down_local, preferred_element_type=jnp.float32),
        "expert",
        split_axis=0,
        concat_axis=0,
        tiled=True,
    )
    summed = jnp.sum(
        returned.reshape(EXPERTS // per_expert, spread, per_expert, CAP, quarter), axis=1
    )
    summed = summed.reshape(EXPERTS * CAP, quarter)
    coefficients = jnp.where(slot_match, mixing[:, :, None], 0.0).reshape(row_count, EXPERTS * CAP)
    moe_part = jnp.dot(
        coefficients, summed, precision=lax.Precision.HIGHEST, preferred_element_type=jnp.float32
    )
    moe_whole = lax.all_gather(moe_part.astype(jnp.bfloat16), "ctx", axis=1, tiled=True)
    return (attn_out, moe_whole)


def solution(mesh):
    return jax.shard_map(
        shards,
        mesh=mesh,
        in_specs=(
            P("expert", None, None),
            P("expert", "ctx", None),
            P("expert"),
            P("expert", None),
            P("expert", None),
            P("expert", None),
            P("expert", None),
            P("ctx", "expert"),
            P("ctx", "expert"),
            P("expert", "ctx"),
        ),
        out_specs=(P("expert", "ctx", None), P("expert", None)),
        check_vma=False,
    )
```

profile of v0, /device:TPU:8, one launch (start us, length us, event | category | flops | bytes accessed | tf_op | source)
XLA Modules:
  0.0 361.9 jit_solution(5321175421044417222)
XLA Ops:
  7.2 0.0 copy-start
  7.2 0.0 all-reduce.3.cloned.1.call-start
  7.2 0.9 copy.43
  8.1 0.1 convert_reduce_fusion
  8.3 0.1 eq.71
  8.4 0.1 eq.74
  8.5 0.1 and.38
  8.6 0.1 and.40
  8.7 0.1 eq.76
  8.8 1.2 convolution_convert_fusion
  10.0 0.2 broadcast_in_dim.79
  10.2 0.3 broadcast_in_dim.80
  10.5 97.0 %all_to_all.10 = bf16[64,1,12,1792]{3,2,1,0:T(8,128)(2,1)S(1)} all-to-all(bf16[64,1,12,1792]{3,2,1,0:T(8,128)(2,1)S(1)} %bitcast.83), channel_id=1, replica_groups=mesh['expert'=64,'ctx'=4] {'expert'}, dimensions={0} | all-to-all | bytes 5505024 | tf_op jit(solution)/shard_map/all_to_all | solution.py:90
  107.5 2.8 fusion.17
  110.2 2.7 fusion.22
  113.0 0.0 all-reduce.3.cloned.1.call-update
  113.0 77.4 %all-reduce.3.cloned.1.call-done = (f32[64,1,12,512]{3,0,2,1:T(8,128)}, f32[64,1,12,512]{3,0,2,1:T(8,128)}) async-done(((f32[64,1,12,512]{3,0,2,1:T(8,128)}, f32[64,1,12,512]{3,0,2,1:T(8,128)}), (f32[64,1,12,512]{3,0,2,1:T(8,128)}, f32[64,1,12,512]{3,0,2,1:T(8,128)})) %all-reduce.3.cloned.1.call-update) | async-done | bytes 3145744 | tf_op jit(solution)/shard_map/psum | solution.py:93
  190.4 3.7 %convolution_bitcast_fusion = f32[64,1,12,1792]{3,0,2,1:T(8,128)S(1)} fusion(bf16[512,1792]{1,0:T(8,128)(2,1)S(1)} %copy-done, f32[64,1,12,512]{3,0,2,1:T(8,128)} %get-tuple-element.195, f32[64,1,12,512]{3,0,2,1:T(8,128)} %get-tuple-element.196), kind=kOutput, calls=%fused_computation.12 | convolution fusion | flops 1411645440 | bytes 10485760 | tf_op jit(solution)/shard_map/sqnf,qfd->sqnd/dot_general | solution.py:96
  194.1 6.8 %copy.46 = f32[64,1,12,1792]{3,1,2,0:T(1,128)} copy(f32[64,1,12,1792]{3,0,2,1:T(8,128)S(1)} %convolution_bitcast_fusion) | data formatting | bytes 11010048 | tf_op jit(solution)/shard_map/sqnf,qfd->sqnd/transpose | solution.py:96
  200.9 10.9 %all-to-all-start.1 = ((f32[64,1,12,1792]{3,1,2,0:T(1,128)}), f32[64,1,12,1792]{3,1,2,0:T(1,128)}, u32[]{:S(2)}, u32[]{:S(2)}) async-start(f32[64,1,12,1792]{3,1,2,0:T(1,128)} %copy.46), calls=%async_computation.1 | async-start | bytes 11010048 | tf_op jit(solution)/shard_map/all_to_all | solution.py:95
  211.8 0.2 all-gather.7.cloned.1.call-start
  212.1 0.2 compare_reduce_fusion
  212.2 0.1 compare_and_fusion
  212.3 0.0 slice-start.1
  212.4 3.8 %fusion.45 = (f32[2,128]{1,0:T(2,128)S(1)}, f32[2,128,2048]{2,1,0:T(8,128)S(1)}) fusion(bf16[2,128,576]{1,2,0:T(8,128)(2,1)S(1)} %copy-done.2, bf16[2,2048,576]{1,2,0:T(8,128)(2,1)} %param.13, pred[2,2048]{1,0:T(4,128)(4,1)S(1)} %compare_and_fusion), kind=kOutput, calls=%fused_computation.66 | convolution fusion | flops 605552384 | bytes 7115776 | tf_op jit(solution)/shard_map/rhi,rti->rht/dot_general | solution.py:45
  216.1 1.3 copy-done.1
  217.4 5.1 %fusion.3 = f32[2,128,512]{2,1,0:T(8,128)} fusion(bf16[2,2048,576]{1,2,0:T(8,128)(2,1)S(1)} %bitcast.82, f32[2,128,2048]{2,1,0:T(8,128)S(1)} %get-tuple-element.202, f32[2,128]{1,0:T(2,128)S(1)} %get-tuple-element.201, pred[2,2048]{1,0:T(4,128)(4,1)S(1)} %compare_and_fusion), kind=kOutput, calls=%fused_computation.10 | convolution fusion | flops 3222274048 | bytes 6824960 | tf_op jit(solution)/shard_map/rht,rtc->rhc/dot_general | solution.py:53
  222.5 0.0 all-gather.7.cloned.1.call-update
  222.6 0.1 copy.44
  222.6 2.1 fusion.16
  224.7 7.8 %all-gather.4 = f32[4,2,128]{2,1,0:T(2,128)S(1)} all-gather(f32[1,2,128]{2,1,0:T(2,128)S(1)} %bitcast.86), channel_id=3, replica_groups=mesh['expert'=64,'ctx'=4] {'ctx'}, dimensions={0}, use_global_device_ids=true | all-gather | bytes 5120 | tf_op jit(solution)/shard_map/all_gather | solution.py:15
  232.6 8.1 %all-gather.3 = f32[4,2,128]{2,1,0:T(2,128)S(1)} all-gather(f32[1,2,128]{2,1,0:T(2,128)S(1)} %bitcast.85), channel_id=2, replica_groups=mesh['expert'=64,'ctx'=4] {'ctx'}, dimensions={0}, use_global_device_ids=true | all-gather | bytes 5120 | tf_op jit(solution)/shard_map/all_gather | solution.py:15
  240.7 0.1 select_reduce_fusion
  240.8 0.2 fusion.33
  241.0 14.7 %all-gather.7.cloned.1.call-done = f32[8,128,512]{2,1,0:T(8,128)} async-done(((f32[2,128,512]{2,1,0:T(8,128)}), f32[8,128,512]{2,1,0:T(8,128)}) %all-gather.7.cloned.1.call-update) | async-done | bytes 2097168 | tf_op jit(solution)/shard_map/all_gather | solution.py:15
  255.7 1.1 slice.14
  256.8 3.8 %while.19 = (s32[]{:T(128)}, f32[2,128]{1,0:T(2,128)S(1)}, f32[2,128]{1,0:T(2,128)S(1)}, f32[2,128,512]{2,1,0:T(8,128)S(1)}, f32[4,2,128]{2,1,0:T(2,128)S(1)}, /...) while((s32[]{:T(128)}, f32[2,128]{1,0:T(2,128)S(1)}, ...), condition=%wide.region_4.5_spmd, body=%wide.region_3.4_spmd.sunk | while | flops 394757 | bytes 1583255 | solution.py:20
  256.8 1.2 fusion.52
  258.1 1.2 fusion.52
  259.3 1.2 fusion.52
  260.6 0.1 constant_dynamic-slice_fusion.1
  260.6 0.7 divide_convert_fusion
  261.4 74.7 %all-to-all-done.1 = f32[64,1,12,1792]{3,1,2,0:T(1,128)} async-done(((f32[64,1,12,1792]{3,1,2,0:T(1,128)}), f32[64,1,12,1792]{3,1,2,0:T(1,128)}, u32[]{:S(2)}, u32[]{:S(2)}) %all-to-all-start.1) | async-done | bytes 5505056 | tf_op jit(solution)/shard_map/all_to_all | solution.py:95
  336.1 3.4 copy.51
  339.5 0.7 bitcast_reduce_fusion
  340.2 2.0 fusion.10
  342.2 12.2 %all_gather.27 = bf16[16,7168]{1,0:T(8,128)(2,1)S(1)} all-gather(bf16[16,1792]{1,0:T(8,128)(2,1)S(1)} %fusion.10), channel_id=1, replica_groups=mesh['expert'=64,'ctx'=4] {'ctx'}, dimensions={1}, use_global_device_ids=true | all-gather | bytes 286720 | tf_op jit(solution)/shard_map/all_gather | solution.py:110
  354.4 0.7 copy.82
  (28 shorter events, 0.2 us)
Async XLA Ops:
  7.2 183.3 %copy-start = (bf16[512,1792]{1,0:T(8,128)(2,1)S(1)}, bf16[512,1792]{1,0:T(8,128)(2,1)}, u32[]{:S(2)}) copy-start(bf16[512,1792]{1,0:T(8,128)(2,1)} %param.21) | copy-start | bytes 5505028
  7.2 183.2 %all-reduce.3.cloned.1.call-start = ((), (), s32[]{:S(2)}) async-start(), calls=%async_computation.3 | async-start | bytes 6291456 | tf_op jit(solution)/shard_map/psum | solution.py:93
  10.5 97.0 %copy-start.6 = (bf16[1792,512]{1,0:T(8,128)(2,1)S(1)}, bf16[1792,512]{1,0:T(8,128)(2,1)}, u32[]{:S(2)}) copy-start(bf16[1792,512]{1,0:T(8,128)(2,1)} %param.19) | copy-start | bytes 5505028
  107.5 2.8 copy-start.7
  200.9 11.1 %copy-start.4 = (s32[2,32]{1,0:T(2,128)S(1)}, s32[2,32]{1,0:T(2,128)}, u32[]{:S(2)}) copy-start(s32[2,32]{1,0:T(2,128)} %param.15) | copy-start | bytes 772
  200.9 11.3 %copy-start.5 = (s32[2]{0:T(128)S(1)}, s32[2]{0:T(128)}, u32[]{:S(2)}) copy-start(s32[2]{0:T(128)} %param.14) | copy-start | bytes 28
  200.9 11.4 %copy-start.2 = (bf16[2,128,576]{1,2,0:T(8,128)(2,1)S(1)}, bf16[2,128,576]{1,2,0:T(8,128)(2,1)}, u32[]{:S(2)}) copy-start(bf16[2,128,576]{1,2,0:T(8,128)(2,1)} %param.12) | copy-start | bytes 884740
  200.9 16.5 %slice-start = ((s8[4718592]{0:T(1024)(128)(4,1)}), s8[524288]{0:T(1024)(128)(4,1)S(1)}, s32[]{:S(2)}) async-start(s8[4718592]{0:T(1024)(128)(4,1)} %bitcast.81), calls=%async_computation.4 | async-start | bytes 1048576
  200.9 135.2 %all-to-all-start.1 = ((f32[64,1,12,1792]{3,1,2,0:T(1,128)}), f32[64,1,12,1792]{3,1,2,0:T(1,128)}, u32[]{:S(2)}, u32[]{:S(2)}) async-start(f32[64,1,12,1792]{3,1,2,0:T(1,128)} %copy.46), calls=%async_computation.1 | async-start | bytes 11010048 | tf_op jit(solution)/shard_map/all_to_all | solution.py:95
  211.8 43.9 %all-gather.7.cloned.1.call-start = ((), (), s32[]{:S(2)}) async-start(), calls=%async_computation.2 | async-start | bytes 2621440 | tf_op jit(solution)/shard_map/all_gather | solution.py:15
  212.3 5.1 %slice-start.1 = ((s8[4718592]{0:T(1024)(128)(4,1)}), s8[4194304]{0:T(1024)(128)(4,1)S(1)}, s32[]{:S(2)}) async-start(s8[4718592]{0:T(1024)(128)(4,1)} %bitcast.81), calls=%async_computation.5 | async-start | bytes 8388608
  216.1 1.3 copy-start.1
  217.4 5.1 %copy-start.3 = (f32[16,8]{0,1:T(8,128)S(1)}, f32[16,8]{0,1:T(8,128)}, u32[]{:S(2)}) copy-start(f32[16,8]{0,1:T(8,128)} %param.18) | copy-start | bytes 1540
Sparse Core Ops, SparseCore 0:
  113.1 77.2 all-reduce.2
  222.7 32.9 all-gather.6
where the time goes:
time: 362 us
  waiting for transfers between devices  167 us (46%)
  blocking collectives  125 us (35%)
  matrix products  21.3 us (6%)
  local copies, waits for them, and re-layouts  15.3 us (4%)
  between operations  14.3 us (4%)
  starting transfers between devices  11.1 us (3%)
  other arithmetic  7.89 us (2%)
    all_to_all x1, blocking collectives, shards(): lax.all_to_all(outgoing, 'expert', split_axis=0, concat_axis=0, tiled=True)  97 us
    psum x1, waiting for transfers between devices, shards(): gate_sum, up_sum = lax.psum((gate_sum, up_sum), 'ctx')  77.4 us
    all_to_all x1, waiting for transfers between devices, shards(): lax.all_to_all(jnp.einsum('sqnf,qfd->sqnd', activated, down_local, prefer...  74.7 us
    all_gather x2, blocking collectives, joined(): gathered = jax.tree.map(lambda a: lax.all_gather(a, axis), part)  16 us
    all_gather x1, waiting for transfers between devices, joined(): gathered = jax.tree.map(lambda a: lax.all_gather(a, axis), part)  14.7 us
    all_gather x1, blocking collectives, shards(): lax.all_gather(moe_part.astype(jnp.bfloat16), 'ctx', axis=1, tiled=True)  12.2 us
    all_to_all x1, starting transfers between devices, shards(): lax.all_to_all(jnp.einsum('sqnf,qfd->sqnd', activated, down_local, prefer...  10.9 us
  transfers between devices with their start and end apart: 3, of which 3 were waited for; matrix products, arithmetic and copies ran while one was open for 5% of the time, Pallas kernels for 0%

commit v1 on v0

v1 whole, which is shorter than its diff:
```python
import jax
import jax.numpy as jnp
from jax import lax
from jax.experimental import pallas as pl
from jax.experimental.pallas import tpu as pltpu
from jax.sharding import PartitionSpec as P

FF = 2048
KV = 512
QK_DIM = 192
EXPERTS = 16
BLOCK = 64
CAP = 12
Z, Y, X = 8, 4, 4
ROWS = 16
QUARTER = 1792
WIDE = QUARTER + 128
UNITS = 512
SLOTS = 192
SHARE = SLOTS // X
SPAN = 2048
HEADS = 128
HEAD_SHARE = HEADS // X
WIDTH = 576
LOW = -1e30
A_CHUNKS = ((0, -1, 1, -2), (2, -3, 3, -4))
B_CHUNKS = ((0, 1), (-1, 2))
F32 = jnp.float32
BF16 = jnp.bfloat16

COPIES = {}


def number(*key):
    return COPIES.setdefault(key, len(COPIES))


for d in (1, 2, 3):
    number("spread_y", d)
    number("slab_y", d)
    number("att", d)
    number("att_top", d)
    number("back_y", d)
    number("last_y", d)
    number("out", d)
    for k in range(4):
        number("sums", k, d)
        number("act", k, d)
for d in range(1, 8):
    number("spread_z", d)
    number("last_z", d)
for s in range(4):
    number("right", s)
    number("left", s)
    number("back_right", s)
    number("back_left", s)
for o in (0, -1, 1, -2, 2, -3, 3, -4):
    number("pass_a", o)
    number("give_a", o)
for o in (0, 1, -1, 2):
    number("pass_b", o)
    number("give_b", o)


def kernel(
    blocks_ref, lengths_ref, routes_ref, route_weights_ref, tokens_hbm, query_hbm, cache_hbm, gate_hbm, up_hbm, down_hbm,
    att_ref, out_ref,
    own, ga, gb, w_gate, w_up, w_down, query, cache,
    att_sum, att_send, att_top, att_got, att_got_top,
    earlier, place, mix, sums, sums_send, sums_got, acts,
    oa, ob, ra, rb, right_send, right_got, left_send, left_got,
    final_a, last_y_got, back_send, back_got, final_b, last_z_send, last_z_got, finals,
    load_sem, send_sem, recv_sem,
):
    index = lax.axis_index("expert")
    x = lax.axis_index("ctx")
    core = lax.rem(index, 2)
    y = lax.rem(index // 2, Y)
    z = index // (2 * Y)
    own_expert = index // (FF // UNITS)
    first, second = core == 0, core == 1

    def at(zz, yy, cc):
        return (zz * (2 * Y) + yy * 2 + cc, x)

    def zo(o):
        return lax.rem(z + o + Z, Z)

    def yo(o):
        return lax.rem(y + o + Y, Y)

    def xo(o):
        return lax.rem(x + o + X, X)

    def copy(key, src, dst, device):
        i = COPIES[key]
        return pltpu.make_async_remote_copy(
            src_ref=src, dst_ref=dst, send_sem=send_sem.at[i], recv_sem=recv_sem.at[i], device_id=device,
            device_id_type=pl.DeviceIdType.MESH,
        )

    to_y = lambda o: at(z, yo(o), core)
    to_z = lambda o: at(zo(o), y, core)
    to_x = lambda o: (index, xo(o))
    sibling = at(z, y, 1 - core)

    def rows16(i):
        return pl.ds(pl.multiple_of(i * ROWS, ROWS), ROWS)

    def load(i, src, dst):
        return pltpu.make_async_copy(src, dst, load_sem.at[i])

    loads = [
        load(0, tokens_hbm.at[:, pl.ds(pl.multiple_of(x * QUARTER, 128), QUARTER)], own.at[:, pl.ds(0, QUARTER)]),
        load(1, query_hbm, query),
        load(2, cache_hbm.at[0], cache.at[0]),
        load(3, cache_hbm.at[1], cache.at[1]),
        load(4, gate_hbm, w_gate),
        load(5, up_hbm, w_up),
        load(6, down_hbm, w_down),
    ]
    for one in loads:
        one.start()

    barrier = pltpu.get_barrier_semaphore()

    def greet(device):
        pl.semaphore_signal(barrier, inc=1, device_id=device, device_id_type=pl.DeviceIdType.MESH)

    for d in (1, 2, 3):
        greet(to_x(d))
        greet(to_y(d))
    greet(sibling)

    @pl.when(first)
    def _():
        greet(to_z(1))
        greet(to_z(-1))

    @pl.when(second)
    def _():
        for d in range(1, Z):
            greet(to_z(d))

    lane = lax.broadcasted_iota(jnp.int32, (ROWS, 128), 1)
    mixing = jnp.zeros((ROWS, 128), F32)
    for k in range(8):
        mixing = jnp.where(lane == routes_ref[:, k : k + 1], route_weights_ref[:, k : k + 1], mixing)
    high = mixing.astype(BF16)
    low = (mixing - high.astype(F32)).astype(BF16)
    low = pltpu.roll(low.astype(F32), EXPERTS, 1)
    own[:, QUARTER:] = (high.astype(F32) + low).astype(BF16)
    row_id = lax.broadcasted_iota(jnp.int32, (256, 256), 0)
    column_id = lax.broadcasted_iota(jnp.int32, (256, 256), 1)
    earlier[...] = jnp.where((row_id // ROWS == column_id // ROWS) & (column_id < row_id), 1.0, 0.0).astype(BF16)
    loads[0].wait()

    @pl.when(first)
    def _():
        ga[z, rows16(y), :] = own[...]
        pl.semaphore_wait(barrier, 9)

    @pl.when(second)
    def _():
        gb[y, rows16(z), :] = own[...]
        pl.semaphore_wait(barrier, 14)

    def spread_y(d):
        return copy(("spread_y", d), own, ga.at[z, rows16(y)], to_y(d))

    def spread_y_in(d):
        return copy(("spread_y", d), own, ga.at[z, rows16(yo(-d))], to_y(d))

    def spread_z(d):
        return copy(("spread_z", d), own, gb.at[y, rows16(z)], to_z(d))

    def spread_z_in(d):
        return copy(("spread_z", d), own, gb.at[y, rows16(zo(-d))], to_z(d))

    def right(s):
        return copy(("right", s), ga.at[zo(-s)], ga.at[zo(-s)], to_z(1))

    def right_in(s):
        return copy(("right", s), ga.at[zo(-s - 1)], ga.at[zo(-s - 1)], to_z(1))

    def left(s):
        return copy(("left", s), ga.at[zo(s)], ga.at[zo(s)], to_z(-1))

    def left_in(s):
        return copy(("left", s), ga.at[zo(s + 1)], ga.at[zo(s + 1)], to_z(-1))

    def pass_a(o):
        return copy(("pass_a", o), ga.at[zo(o)], ga.at[zo(o)], sibling)

    def slab_y(d):
        return copy(("slab_y", d), gb.at[y], gb.at[y], to_y(d))

    def slab_y_in(d):
        return copy(("slab_y", d), gb.at[yo(-d)], gb.at[yo(-d)], to_y(d))

    def pass_b(o):
        return copy(("pass_b", o), gb.at[yo(o)], gb.at[yo(o)], sibling)

    @pl.when(first)
    def _():
        for d in (2, 1, 3):
            spread_y(d).start()

    @pl.when(second)
    def _():
        for d in (4, 3, 5, 2, 6, 1, 7):
            spread_z(d).start()

    def attend(s):
        position = x * SPAN + lax.broadcasted_iota(jnp.int32, (1, SPAN), 1)
        owning = position // BLOCK
        chosen = owning == blocks_ref[s, 0]
        for i in range(1, 32):
            chosen = chosen | (owning == blocks_ref[s, i])
        chosen = chosen & (position < lengths_ref[s])
        scores = lax.dot_general(query[s], cache[s], (((1,), (1,)), ((), ())), preferred_element_type=F32)
        scores = jnp.where(chosen, scores * QK_DIM ** (-0.5), LOW)
        peak = jnp.max(scores, axis=1, keepdims=True)
        weights = jnp.exp(scores - peak)
        total = jnp.sum(weights, axis=1, keepdims=True)
        latent = jnp.dot(weights.astype(BF16), cache[s, :, :KV], preferred_element_type=F32)
        half = lax.broadcasted_iota(jnp.int32, (HEADS, 128), 1) < 64
        top = jnp.where(half, peak, total)
        for i in range(X):
            part = slice(i * HEAD_SHARE, (i + 1) * HEAD_SHARE)
            att_sum[i, s] = latent[part]
            att_send[i, s] = latent[part].astype(BF16)
            att_top[i, s] = top[part]

    def att_copy(d):
        return copy(("att", d), att_send.at[xo(d)], att_got.at[d - 1], to_x(d))

    def att_top_copy(d):
        return copy(("att_top", d), att_top.at[xo(d)], att_got_top.at[d - 1], to_x(d))

    def attend_end():
        for d in (1, 2, 3):
            att_copy(d).wait_recv()
            att_top_copy(d).wait_recv()
        tops = [att_top[x]] + [att_got_top[i] for i in range(3)]
        parts = [att_sum[x]] + [att_got[i].astype(F32) for i in range(3)]
        peaks = [t[:, :, 0:1] for t in tops]
        highest = jnp.maximum(jnp.maximum(peaks[0], peaks[1]), jnp.maximum(peaks[2], peaks[3]))
        factors = [jnp.exp(p - highest) for p in peaks]
        total = sum(f * t[:, :, 64:65] for f, t in zip(factors, tops))
        whole = sum(f * p for f, p in zip(factors, parts))
        att_ref[...] = (whole / total).astype(BF16)

    def slabs(k):
        if k % 2 == 0:
            return [ga.at[zo(o)] for o in A_CHUNKS[k // 2]]
        return [gb.at[yo(o)] for o in B_CHUNKS[k // 2]]

    def chunk(k):
        rows = jnp.concatenate([r[...] for r in slabs(k)], axis=0)
        coefficients = rows[:, QUARTER:].astype(F32)
        lanes = lax.broadcasted_iota(jnp.int32, (256, 128), 1)
        mine = (lanes == own_expert) | (lanes == own_expert + EXPERTS)
        share = jnp.sum(jnp.where(mine, coefficients, 0.0), axis=1, keepdims=True)
        hit = share > 0
        hits = jnp.broadcast_to(jnp.where(hit, 1.0, 0.0), (256, 128)).astype(BF16)
        rank = jnp.dot(earlier[...], hits, preferred_element_type=F32)[:, :1].astype(jnp.int32)
        slot = rank + CAP * (lax.broadcasted_iota(jnp.int32, (256, 1), 0) // ROWS)
        slot = jnp.where(hit, slot, -1)
        placing = jnp.where(slot == lax.broadcasted_iota(jnp.int32, (256, SLOTS), 1), 1.0, 0.0).astype(BF16)
        place[k] = placing
        mix[k] = jnp.broadcast_to(share, (256, 128))
        packed = lax.dot_general(
            placing, rows[:, :QUARTER], (((0,), (0,)), ((), ())), preferred_element_type=F32
        ).astype(BF16)
        for half, weight in enumerate((w_gate, w_up)):
            part = jnp.dot(packed, weight[...], preferred_element_type=F32)
            for i in range(X):
                columns = slice(half * UNITS, (half + 1) * UNITS)
                one = part[i * SHARE : (i + 1) * SHARE]
                sums[k, i, :, columns] = one
                sums_send[k, i, :, columns] = one.astype(BF16)
        for d in (2, 1, 3):
            sums_copy(k, d).start()

    def sums_copy(k, d):
        return copy(("sums", k, d), sums_send.at[k, xo(d)], sums_got.at[k, d - 1], to_x(d))

    def act_copy(k, d):
        return copy(("act", k, d), acts.at[k, x], acts.at[k, x], to_x(d))

    def act_copy_in(k, d):
        return copy(("act", k, d), acts.at[k, xo(-d)], acts.at[k, xo(-d)], to_x(d))

    def activate(k):
        for d in (1, 2, 3):
            sums_copy(k, d).wait_recv()
        both = sums[k, x]
        for i in range(3):
            both = both + sums_got[k, i].astype(F32)
        gate, up = both[:, :UNITS], both[:, UNITS:]
        acts[k, x] = (gate / (1.0 + jnp.exp(-gate)) * up).astype(BF16)
        for d in (2, 1, 3):
            act_copy(k, d).start()

    def give_a(o):
        return copy(("give_a", o), oa.at[zo(o)], ra.at[zo(o)], sibling)

    def give_b(o):
        return copy(("give_b", o), ob.at[yo(o)], rb.at[yo(o)], sibling)

    def finish(k):
        for d in (1, 2, 3):
            act_copy_in(k, d).wait_recv()
        inside = jnp.concatenate([acts[k, i] for i in range(X)], axis=0)
        spread = jnp.dot(place[k], inside, preferred_element_type=F32).astype(BF16)
        result = jnp.dot(spread, w_down[...], preferred_element_type=F32) * mix[k][:, :1]
        if k % 2 == 0:
            for i, o in enumerate(A_CHUNKS[k // 2]):
                oa[zo(o)] = result[i * 64 : (i + 1) * 64]

            @pl.when(second)
            def _():
                for o in A_CHUNKS[k // 2]:
                    give_a(o).start()
        else:
            for i, o in enumerate(B_CHUNKS[k // 2]):
                ob[yo(o)] = result[i * 128 : (i + 1) * 128]

            @pl.when(first)
            def _():
                for o in B_CHUNKS[k // 2]:
                    give_b(o).start()

    loads[1].wait()
    loads[2].wait()
    attend(0)

    @pl.when(first)
    def _():
        for d in (1, 2, 3):
            spread_y_in(d).wait_recv()
        right(0).start()
        left(0).start()
        pass_a(0).start()

    @pl.when(second)
    def _():
        for d in range(1, Z):
            spread_z_in(d).wait_recv()
        for d in (2, 1, 3):
            slab_y(d).start()
        pass_b(0).start()

    loads[3].wait()
    attend(1)
    for d in (2, 1, 3):
        att_copy(d).start()
        att_top_copy(d).start()

    @pl.when(first)
    def _():
        right_in(0).wait_recv()
        left_in(0).wait_recv()
        right(1).start()
        left(1).start()
        pass_a(-1).start()
        pass_a(1).start()
        right_in(1).wait_recv()
        left_in(1).wait_recv()
        right(2).start()
        left(2).start()
        pass_a(-2).start()
        pass_a(2).start()

    @pl.when(second)
    def _():
        for o in A_CHUNKS[0]:
            pass_a(o).wait_recv()

    loads[4].wait()
    loads[5].wait()
    chunk(0)

    @pl.when(first)
    def _():
        right_in(2).wait_recv()
        left_in(2).wait_recv()
        right(3).start()
        pass_a(-3).start()
        pass_a(3).start()
        for o in B_CHUNKS[0]:
            pass_b(o).wait_recv()

    @pl.when(second)
    def _():
        for d in (1, 2, 3):
            slab_y_in(d).wait_recv()
            pass_b({1: -1, 2: 2, 3: 1}[d]).start()

    chunk(1)
    activate(0)

    @pl.when(first)
    def _():
        right_in(3).wait_recv()
        pass_a(-4).start()

    @pl.when(second)
    def _():
        for o in A_CHUNKS[1]:
            pass_a(o).wait_recv()

    chunk(2)
    loads[6].wait()
    finish(0)
    activate(1)

    @pl.when(first)
    def _():
        for o in B_CHUNKS[1]:
            pass_b(o).wait_recv()

    chunk(3)
    activate(2)
    finish(1)
    attend_end()
    activate(3)
    finish(2)
    finish(3)

    def back_right(s):
        return copy(("back_right", s), right_send.at[s], right_got.at[s], to_z(1))

    def back_left(s):
        return copy(("back_left", s), left_send.at[s], left_got.at[s], to_z(-1))

    def back_y(d):
        return copy(("back_y", d), back_send.at[d - 1], back_got.at[d - 1], to_y(d))

    def last_y(d):
        return copy(("last_y", d), final_a.at[yo(d)], last_y_got.at[d - 1], to_y(d))

    def last_z(d):
        return copy(("last_z", d), last_z_send.at[zo(d)], last_z_got.at[d - 1], to_z(d))

    def out_copy(d):
        return copy(("out", d), finals.at[x], finals.at[x], to_x(d))

    def out_copy_in(d):
        return copy(("out", d), finals.at[xo(-d)], finals.at[xo(-d)], to_x(d))

    @pl.when(first)
    def _():
        for o in A_CHUNKS[0] + A_CHUNKS[1]:
            give_a(o).wait_recv()

        def chip(o):
            return oa[zo(o)] + ra[zo(o)]

        right_send[0] = chip(4 - Z).astype(BF16)
        back_right(0).start()
        left_send[0] = chip(-3).astype(BF16)
        back_left(0).start()
        for s in (1, 2, 3):
            back_right(s - 1).wait_recv()
            right_send[s] = (chip(4 - s) + right_got[s - 1].astype(F32)).astype(BF16)
            back_right(s).start()
            if s < 3:
                back_left(s - 1).wait_recv()
                left_send[s] = (chip(s - 3) + left_got[s - 1].astype(F32)).astype(BF16)
                back_left(s).start()
        back_left(2).wait_recv()
        back_right(3).wait_recv()
        whole = chip(0) + right_got[3].astype(F32) + left_got[2].astype(F32)
        for i in range(Y):
            final_a[i] = whole[i * ROWS : (i + 1) * ROWS]
        for d in (2, 1, 3):
            last_y(d).start()
        for d in (1, 2, 3):
            last_y(d).wait_recv()
        finals[x] = (final_a[y] + last_y_got[0] + last_y_got[1] + last_y_got[2]).astype(BF16)

    @pl.when(second)
    def _():
        for o in B_CHUNKS[0] + B_CHUNKS[1]:
            give_b(o).wait_recv()

        def chip(o):
            return ob[yo(o)] + rb[yo(o)]

        for d in (2, 1, 3):
            back_send[d - 1] = chip(d if d < 3 else -1).astype(BF16)
            back_y(d).start()
        for d in (1, 2, 3):
            back_y(d).wait_recv()
        whole = chip(0)
        for i in range(3):
            whole = whole + back_got[i].astype(F32)
        for i in range(Z):
            one = whole[i * ROWS : (i + 1) * ROWS]
            final_b[i] = one
            last_z_send[i] = one.astype(BF16)
        for d in (4, 3, 5, 2, 6, 1, 7):
            last_z(d).start()
        total = final_b[z]
        for d in range(1, Z):
            last_z(d).wait_recv()
            total = total + last_z_got[d - 1].astype(F32)
        finals[x] = total.astype(BF16)

    for d in (2, 1, 3):
        out_copy(d).start()
    for d in (1, 2, 3):
        out_copy_in(d).wait_recv()
    for i in range(X):
        out_ref[:, i * QUARTER : (i + 1) * QUARTER] = finals[i]

    for d in (1, 2, 3):
        att_copy(d).wait_send()
        att_top_copy(d).wait_send()
        out_copy(d).wait_send()
        for k in range(4):
            sums_copy(k, d).wait_send()
            act_copy(k, d).wait_send()

    @pl.when(first)
    def _():
        for d in (1, 2, 3):
            spread_y(d).wait_send()
            last_y(d).wait_send()
        for s in range(4):
            right(s).wait_send()
            back_right(s).wait_send()
            if s < 3:
                left(s).wait_send()
                back_left(s).wait_send()
        for o in A_CHUNKS[0] + A_CHUNKS[1]:
            pass_a(o).wait_send()
        for o in B_CHUNKS[0] + B_CHUNKS[1]:
            give_b(o).wait_send()

    @pl.when(second)
    def _():
        for d in range(1, Z):
            spread_z(d).wait_send()
            last_z(d).wait_send()
        for d in (1, 2, 3):
            slab_y(d).wait_send()
            back_y(d).wait_send()
        for o in B_CHUNKS[0] + B_CHUNKS[1]:
            pass_b(o).wait_send()
        for o in A_CHUNKS[0] + A_CHUNKS[1]:
            give_a(o).wait_send()


def shards(query, cache, lengths, blocks, moe_tokens, routes, route_weights, w_gate, w_up, w_down):
    smem = pl.BlockSpec(memory_space=pltpu.SMEM)
    vmem = pl.BlockSpec(memory_space=pltpu.VMEM)
    hbm = pl.BlockSpec(memory_space=pl.ANY)
    scratch = lambda *shape: pltpu.VMEM(shape, BF16)
    wide = lambda *shape: pltpu.VMEM(shape, F32)
    return pl.pallas_call(
        kernel,
        out_shape=(
            jax.ShapeDtypeStruct((2, HEAD_SHARE, KV), BF16),
            jax.ShapeDtypeStruct((ROWS, X * QUARTER), BF16),
        ),
        in_specs=[smem, smem, vmem, vmem] + [hbm] * 6,
        out_specs=(vmem, vmem),
        scratch_shapes=[
            scratch(ROWS, WIDE),
            scratch(Z, 64, WIDE),
            scratch(Y, 128, WIDE),
            scratch(QUARTER, UNITS),
            scratch(QUARTER, UNITS),
            scratch(UNITS, QUARTER),
            scratch(2, HEADS, WIDTH),
            scratch(2, SPAN, WIDTH),
            wide(X, 2, HEAD_SHARE, KV),
            scratch(X, 2, HEAD_SHARE, KV),
            wide(X, 2, HEAD_SHARE, 128),
            scratch(3, 2, HEAD_SHARE, KV),
            wide(3, 2, HEAD_SHARE, 128),
            scratch(256, 256),
            scratch(4, 256, SLOTS),
            wide(4, 256, 128),
            wide(4, X, SHARE, 2 * UNITS),
            scratch(4, X, SHARE, 2 * UNITS),
            scratch(4, 3, SHARE, 2 * UNITS),
            scratch(4, X, SHARE, UNITS),
            wide(Z, 64, QUARTER),
            wide(Y, 128, QUARTER),
            wide(Z, 64, QUARTER),
            wide(Y, 128, QUARTER),
            scratch(4, 64, QUARTER),
            scratch(4, 64, QUARTER),
            scratch(3, 64, QUARTER),
            scratch(3, 64, QUARTER),
            wide(Y, ROWS, QUARTER),
            wide(3, ROWS, QUARTER),
            scratch(3, 128, QUARTER),
            scratch(3, 128, QUARTER),
            wide(Z, ROWS, QUARTER),
            scratch(Z, ROWS, QUARTER),
            scratch(7, ROWS, QUARTER),
            scratch(X, ROWS, QUARTER),
            pltpu.SemaphoreType.DMA((7,)),
            pltpu.SemaphoreType.DMA((len(COPIES),)),
            pltpu.SemaphoreType.DMA((len(COPIES),)),
        ],
        compiler_params=pltpu.CompilerParams(
            collective_id=0, has_side_effects=True, vmem_limit_bytes=62 * 1024 * 1024
        ),
    )(blocks, lengths, routes, route_weights, moe_tokens, query, cache, w_gate, w_up, w_down)


def solution(mesh):
    return jax.shard_map(
        shards,
        mesh=mesh,
        in_specs=(
            P("expert", None, None),
            P("expert", "ctx", None),
            P("expert"),
            P("expert", None),
            P("expert", None),
            P("expert", None),
            P("expert", None),
            P("ctx", "expert"),
            P("ctx", "expert"),
            P("expert", "ctx"),
        ),
        out_specs=(P("expert", "ctx", None), P("expert", None)),
        check_vma=False,
    )
```

time: 362 us -> 112 us (0.31)
  waiting for transfers between devices: 167 us -> 0 us
  blocking collectives: 125 us -> 0 us
  Pallas kernels: 0 us -> 95.1 us
  matrix products: 21.3 us -> 0 us
  between operations: 14.3 us -> 0.64 us
  starting transfers between devices: 11.1 us -> 0 us
  other arithmetic: 7.89 us -> 0 us
    all_to_all x1 -> x0, blocking collectives: 97 us -> none  [shards(): lax.all_to_all(outgoing, 'expert', split_axis=0, concat_axis=0, tiled=True)]
    pallas_call x0 -> x1, Pallas kernels: none -> 95.1 us  [shards(): pl.pallas_call(kernel, out_shape=(jax.ShapeDtypeStruct((2, HEAD_SHARE, KV...]
    psum x1 -> x0, waiting for transfers between devices: 77.4 us -> none  [shards(): gate_sum, up_sum = lax.psum((gate_sum, up_sum), 'ctx')]
    all_to_all x1 -> x0, waiting for transfers between devices: 74.7 us -> none  [shards(): lax.all_to_all(jnp.einsum('sqnf,qfd->sqnd', activated, down_local, prefer...]
    all_gather x3 -> x0, blocking collectives: 28.1 us -> none  [the longest x2 16 us: joined(): gathered = jax.tree.map(lambda a: lax.all_gather(a, axis), part)]
    dot_general x7 -> x0, matrix products: 21.3 us -> none  [the longest x1 5.09 us: shards(): jnp.einsum('rht,rtc->rhc', weights, latent_values, precision=lax.Precisio...]
    all_gather x1 -> x0, waiting for transfers between devices: 14.7 us -> none  [joined(): gathered = jax.tree.map(lambda a: lax.all_gather(a, axis), part)]
    all_to_all x1 -> x0, starting transfers between devices: 10.9 us -> none  [shards(): lax.all_to_all(jnp.einsum('sqnf,qfd->sqnd', activated, down_local, prefer...]
  transfers between devices with their start and end apart: 3 -> 0, of which waited for: 3 -> 0; matrix products, arithmetic and copies ran while one was open for 5% -> 0% of each run, Pallas kernels for 0% -> 0%
where the time goes in v1:
time: 112 us; the launch traced here: 111 us
  Pallas kernels  95.1 us (85%)
  local copies, waits for them, and re-layouts  15.4 us (14%)
    pallas_call x1, Pallas kernels, shards(): pl.pallas_call(kernel, out_shape=(jax.ShapeDtypeStruct((2, HEAD_SHARE, KV...  95.1 us
    unnamed x6, local copies, waits for them, and re-layouts  15.4 us

profile of v1, /device:TPU:8, one launch (start us, length us, event | category | flops | bytes accessed | tf_op | source)
XLA Modules:
  0.0 111.1 jit_solution(17803728014515573725)
XLA Ops:
  0.6 1.4 %copy.12.routes_ref = s32[16,8]{1,0:T(8,128)} copy(s32[16,8]{0,1:T(8,128)} %param.15) | data formatting | bytes 1024 | tf_op args[5]
  2.0 1.4 %copy.13.route_weights_ref = f32[16,8]{1,0:T(8,128)} copy(f32[16,8]{0,1:T(8,128)} %param.16) | data formatting | bytes 1024 | tf_op args[6]
  3.3 1.9 %copy.14.query_hbm = bf16[2,128,576]{2,1,0:T(8,128)(2,1)} copy(bf16[2,128,576]{1,2,0:T(8,128)(2,1)} %param.10) | data formatting | bytes 589824 | tf_op args[0]
  5.2 7.7 %copy.15.cache_hbm = bf16[2,2048,576]{2,1,0:T(8,128)(2,1)} copy(bf16[2,2048,576]{1,2,0:T(8,128)(2,1)} %param.11) | data formatting | bytes 9437184 | tf_op args[1]
  12.9 95.1 %shard_map.113 = (bf16[2,32,512]{2,1,0:T(8,128)(2,1)}, bf16[16,7168]{1,0:T(8,128)(2,1)}) custom-call(s32[2,32]{1,0:T(2,128)} %blocks_ref.1, s32[2]{0:T(128)} %lengths_ref.1, s32[16,8]{1,0:T(8,128)} %copy.12.routes_ref, f32[16,8]{1,0:T(8,128)} %copy.13.route_weights_ref, bf16[16,7168]{1,0:T(8,128)(2,1)} %tokens_hbm.1, bf16[2,128,576]{2,1,0:T(8,128)(2,1)} %copy.14.query_hbm, ...), custom_call_target="tpu_custom_call" | custom-call | tf_op jit(solution)/shard_map/pallas_call | solution.py:563
  108.0 1.5 %copy.18 = bf16[2,32,512]{2,1,0:T(8,128)(2,1)} copy(bf16[2,32,512]{2,1,0:T(8,128)(2,1)} %get-tuple-element.4) | data formatting | bytes 131072
  109.4 1.6 %copy.19 = bf16[16,7168]{1,0:T(8,128)(2,1)} copy(bf16[16,7168]{1,0:T(8,128)(2,1)} %get-tuple-element.5) | data formatting | bytes 458752

commit v2 on v0

v2 whole, which is shorter than its diff:
```python
import jax
import jax.numpy as jnp
from jax import lax
from jax.experimental import pallas as pl
from jax.experimental.pallas import tpu as pltpu
from jax.sharding import PartitionSpec as P

FF = 2048
KV = 512
QK_DIM = 192
EXPERTS = 16
BLOCK = 64
CAP = 12
Z, Y, X = 8, 4, 4
ROWS = 16
QUARTER = 1792
WIDE = QUARTER + 128
UNITS = 512
SLOTS = Y * 2 * CAP
SHARE = UNITS // X
SPAN = 2048
HEADS = 128
HEAD_SHARE = HEADS // X
WIDTH = 576
LOW = -1e30
PLANES = (0, 1, -1, 2, -2, 3, -3, 4)
CHUNKS = len(PLANES)
PLACE = {o: k for k, o in enumerate(PLANES)}
CHUNK_ROWS = Y * 2 * ROWS
F32 = jnp.float32
BF16 = jnp.bfloat16

COPIES = {}


def number(*key):
    return COPIES.setdefault(key, len(COPIES))


for d in (1, 2, 3):
    number("att", d)
    number("att_top", d)
    number("out", d)
    for k in range(CHUNKS):
        number("sums", k, d)
        number("act", k, d)
        number("back_y", k, d)
    for o in PLACE:
        number("fan", o, d)
for o in PLACE:
    if o:
        number("spread", o)
        number("last_z", o)
for k in range(CHUNKS):
    number("pass", k)
    number("give", k)


def kernel(
    blocks_ref, lengths_ref, routes_ref, route_weights_ref, tokens_hbm, query_hbm, cache_hbm, gate_hbm, up_hbm, down_hbm,
    att_ref, out_ref,
    own, rows_all, w_gate, w_up, w_down, query, cache,
    att_sum, att_send, att_top, att_got, att_got_top,
    earlier, place, mix, sums, sums_send, sums_got, acts,
    results, given, chips, chips_send, chips_got, final_own, last_send, last_got, finals,
    load_sem, send_sem, recv_sem,
):
    index = lax.axis_index("expert")
    x = lax.axis_index("ctx")
    core = lax.rem(index, 2)
    y = lax.rem(index // 2, Y)
    z = index // (2 * Y)
    own_expert = index // (FF // UNITS)

    def at(zz, yy, cc):
        return (zz * (2 * Y) + yy * 2 + cc, x)

    def zo(o):
        return lax.rem(z + o + Z, Z)

    def yo(o):
        return lax.rem(y + o + Y, Y)

    def xo(o):
        return lax.rem(x + o + X, X)

    def copy(key, src, dst, device):
        i = COPIES[key]
        return pltpu.make_async_remote_copy(
            src_ref=src, dst_ref=dst, send_sem=send_sem.at[i], recv_sem=recv_sem.at[i], device_id=device,
            device_id_type=pl.DeviceIdType.MESH,
        )

    to_y = lambda o: at(z, yo(o), core)
    to_z = lambda o: at(zo(o), y, core)
    to_x = lambda o: (index, xo(o))
    sibling = at(z, y, 1 - core)

    def load(i, src, dst):
        return pltpu.make_async_copy(src, dst, load_sem.at[i])

    loads = [
        load(0, tokens_hbm.at[:, pl.ds(pl.multiple_of(x * QUARTER, 128), QUARTER)], own.at[:, pl.ds(0, QUARTER)]),
        load(1, query_hbm, query),
        load(2, cache_hbm.at[0], cache.at[0]),
        load(3, cache_hbm.at[1], cache.at[1]),
        load(4, gate_hbm, w_gate),
        load(5, up_hbm, w_up),
        load(6, down_hbm, w_down),
    ]
    for one in loads:
        one.start()

    barrier = pltpu.get_barrier_semaphore()

    def greet(device):
        pl.semaphore_signal(barrier, inc=1, device_id=device, device_id_type=pl.DeviceIdType.MESH)

    for d in (1, 2, 3):
        greet(to_x(d))
        greet(to_y(d))
    greet(sibling)

    for d in range(1, Z):
        greet(to_z(d))

    expert_id = lax.broadcasted_iota(jnp.int32, (EXPERTS, ROWS), 0)
    mixing = jnp.zeros((EXPERTS, ROWS), F32)
    for k in range(8):
        mixing = jnp.where(expert_id == routes_ref[k : k + 1, :], route_weights_ref[k : k + 1, :], mixing)
    high = mixing.astype(BF16)
    low = (mixing - high.astype(F32)).astype(BF16)
    to_row = lax.broadcasted_iota(jnp.int32, (EXPERTS, 128), 0)
    to_lane = lax.broadcasted_iota(jnp.int32, (EXPERTS, 128), 1)
    turned = [
        lax.dot_general(
            part, jnp.where(to_lane == to_row + shift, 1.0, 0.0).astype(BF16), (((0,), (0,)), ((), ())),
            preferred_element_type=F32,
        )
        for part, shift in ((high, 0), (low, EXPERTS))
    ]
    own[:, QUARTER:] = (turned[0] + turned[1]).astype(BF16)
    row_id = lax.broadcasted_iota(jnp.int32, (CHUNK_ROWS, CHUNK_ROWS), 0)
    column_id = lax.broadcasted_iota(jnp.int32, (CHUNK_ROWS, CHUNK_ROWS), 1)
    earlier[...] = jnp.where((row_id // ROWS == column_id // ROWS) & (column_id < row_id), 1.0, 0.0).astype(BF16)
    loads[0].wait()

    rows_all[0, y, core] = own[...]
    pl.semaphore_wait(barrier, 14)

    def spread(o):
        k = PLACE[o]
        return copy(("spread", o), own, rows_all.at[k, y, core], to_z(-o))

    def fan(o, d):
        k = PLACE[o]
        return copy(("fan", o, d), rows_all.at[k, y, core], rows_all.at[k, y, core], to_y(d))

    def fan_in(o, d):
        k = PLACE[o]
        return copy(("fan", o, d), rows_all.at[k, yo(-d), core], rows_all.at[k, yo(-d), core], to_y(d))

    def pass_on(k):
        return copy(("pass", k), rows_all.at[k, :, core], rows_all.at[k, :, core], sibling)

    def pass_in(k):
        return copy(("pass", k), rows_all.at[k, :, 1 - core], rows_all.at[k, :, 1 - core], sibling)

    def fan_out(k):
        o = PLANES[k]
        if o:
            spread(o).wait_recv()
        for d in (1, 3, 2):
            fan(o, d).start()

    def gather(k):
        for d in (1, 3, 2):
            fan_in(PLANES[k], d).wait_recv()
        pass_on(k).start()

    fan_out(0)
    spread(1).start()
    spread(-1).start()

    def attend(s):
        position = x * SPAN + lax.broadcasted_iota(jnp.int32, (1, SPAN), 1)
        owning = position // BLOCK
        chosen = owning == blocks_ref[s, 0]
        for i in range(1, 32):
            chosen = chosen | (owning == blocks_ref[s, i])
        chosen = chosen & (position < lengths_ref[s])
        scores = lax.dot_general(query[s], cache[s], (((0,), (0,)), ((), ())), preferred_element_type=F32)
        scores = jnp.where(chosen, scores * QK_DIM ** (-0.5), LOW)
        peak = jnp.max(scores, axis=1, keepdims=True)
        weights = jnp.exp(scores - peak)
        total = jnp.sum(weights, axis=1, keepdims=True)
        latent = lax.dot_general(
            weights.astype(BF16), cache[s, :KV], (((1,), (1,)), ((), ())), preferred_element_type=F32
        )
        half = lax.broadcasted_iota(jnp.int32, (HEADS, 128), 1) < 64
        top = jnp.where(half, peak, total)
        for i in range(X):
            part = slice(i * HEAD_SHARE, (i + 1) * HEAD_SHARE)
            att_sum[i, s] = latent[part]
            att_send[i, s] = latent[part].astype(BF16)
            att_top[i, s] = top[part]

    def att_copy(d):
        return copy(("att", d), att_send.at[xo(d)], att_got.at[d - 1], to_x(d))

    def att_top_copy(d):
        return copy(("att_top", d), att_top.at[xo(d)], att_got_top.at[d - 1], to_x(d))

    def attend_end():
        for d in (1, 2, 3):
            att_copy(d).wait_recv()
            att_top_copy(d).wait_recv()
        tops = [att_top[x]] + [att_got_top[i] for i in range(3)]
        parts = [att_sum[x]] + [att_got[i].astype(F32) for i in range(3)]
        peaks = [t[:, :, 0:1] for t in tops]
        highest = jnp.maximum(jnp.maximum(peaks[0], peaks[1]), jnp.maximum(peaks[2], peaks[3]))
        factors = [jnp.exp(p - highest) for p in peaks]
        total = sum(f * t[:, :, 64:65] for f, t in zip(factors, tops))
        whole = sum(f * p for f, p in zip(factors, parts))
        att_ref[...] = (whole / total).astype(BF16)

    def chunk(k):
        pass_in(k).wait_recv()
        rows = rows_all[k].reshape(CHUNK_ROWS, WIDE)
        coefficients = rows[:, QUARTER:].astype(F32)
        lanes = lax.broadcasted_iota(jnp.int32, (CHUNK_ROWS, 128), 1)
        mine = (lanes == own_expert) | (lanes == own_expert + EXPERTS)
        share = jnp.sum(jnp.where(mine, coefficients, 0.0), axis=1, keepdims=True)
        hit = share > 0
        hits = jnp.broadcast_to(jnp.where(hit, 1.0, 0.0), (CHUNK_ROWS, 128)).astype(BF16)
        rank = jnp.dot(earlier[...], hits, preferred_element_type=F32)[:, :1].astype(jnp.int32)
        slot = rank + CAP * (lax.broadcasted_iota(jnp.int32, (CHUNK_ROWS, 1), 0) // ROWS)
        slot = jnp.where(hit, slot, -1)
        placing = jnp.where(slot == lax.broadcasted_iota(jnp.int32, (CHUNK_ROWS, SLOTS), 1), 1.0, 0.0).astype(BF16)
        place[k] = placing
        mix[k] = jnp.broadcast_to(share, (CHUNK_ROWS, 128))
        packed = lax.dot_general(
            placing, rows[:, :QUARTER], (((0,), (0,)), ((), ())), preferred_element_type=F32
        ).astype(BF16)
        for half, weight in enumerate((w_gate, w_up)):
            part = jnp.dot(packed, weight[...], preferred_element_type=F32)
            for i in range(X):
                one = part[:, i * SHARE : (i + 1) * SHARE]
                sums[k, i, :, half * SHARE : (half + 1) * SHARE] = one
                sums_send[k, i, :, half * SHARE : (half + 1) * SHARE] = one.astype(BF16)
        for d in (1, 3, 2):
            sums_copy(k, d).start()

    def sums_copy(k, d):
        return copy(("sums", k, d), sums_send.at[k, xo(d)], sums_got.at[k, d - 1], to_x(d))

    def act_copy(k, d):
        return copy(("act", k, d), acts.at[k, x], acts.at[k, x], to_x(d))

    def act_copy_in(k, d):
        return copy(("act", k, d), acts.at[k, xo(-d)], acts.at[k, xo(-d)], to_x(d))

    def activate(k):
        for d in (1, 2, 3):
            sums_copy(k, d).wait_recv()
        both = sums[k, x]
        for i in range(3):
            both = both + sums_got[k, i].astype(F32)
        gate, up = both[:, :SHARE], both[:, SHARE:]
        acts[k, x] = (gate / (1.0 + jnp.exp(-gate)) * up).astype(BF16)
        for d in (1, 3, 2):
            act_copy(k, d).start()

    def give(k):
        return copy(("give", k), results.at[k, :, 1 - core], given.at[k], sibling)

    def finish(k):
        for d in (1, 2, 3):
            act_copy_in(k, d).wait_recv()
        inside = jnp.concatenate([acts[k, i] for i in range(X)], axis=1)
        spread_out = jnp.dot(place[k], inside, preferred_element_type=F32).astype(BF16)
        result = jnp.dot(spread_out, w_down[...], preferred_element_type=F32) * mix[k][:, :1]
        results[k] = result.reshape(Y, 2, ROWS, QUARTER)
        give(k).start()

    def back_y(k, d):
        return copy(("back_y", k, d), chips_send.at[k, yo(d)], chips_got.at[k, d - 1], to_y(d))

    def last_z(o):
        k = PLACE[o]
        return copy(("last_z", o), last_send.at[k], last_got.at[k], to_z(o))

    def out_copy(d):
        return copy(("out", d), finals.at[x], finals.at[x], to_x(d))

    def out_copy_in(d):
        return copy(("out", d), finals.at[xo(-d)], finals.at[xo(-d)], to_x(d))

    def return_y(k):
        give(k).wait_recv()
        for j in range(Y):
            one = results[k, j, core] + given[k, j]
            chips[k, j] = one
            chips_send[k, j] = one.astype(BF16)
        for d in (1, 3, 2):
            back_y(k, d).start()

    def return_z(k):
        for d in (1, 3, 2):
            back_y(k, d).wait_recv()
        one = chips[k, y]
        for j in range(3):
            one = one + chips_got[k, j].astype(F32)
        if k:
            last_send[k] = one.astype(BF16)
            last_z(PLANES[k]).start()
        else:
            final_own[...] = one

    def spread_next(sent, following):
        for o in sent:
            spread(o).wait_send()
        for o in following:
            spread(o).start()

    loads[1].wait()
    loads[2].wait()
    attend(0)
    spread_next((1, -1), (2, -2))
    fan_out(1)
    fan_out(2)
    loads[3].wait()
    attend(1)
    for d in (1, 3, 2):
        att_copy(d).start()
        att_top_copy(d).start()
    spread_next((2, -2), (3, -3))
    gather(0)
    loads[4].wait()
    loads[5].wait()
    for t in range(CHUNKS + 7):
        if t + 3 < CHUNKS:
            fan_out(t + 3)
        if t == 0:
            spread_next((3, -3), (4,))
        if t + 1 < CHUNKS:
            gather(t + 1)
        if t < CHUNKS:
            chunk(t)
        if t == 3:
            loads[6].wait()
        if 0 <= t - 2 < CHUNKS:
            activate(t - 2)
        if 0 <= t - 4 < CHUNKS:
            finish(t - 4)
        if 0 <= t - 5 < CHUNKS:
            return_y(t - 5)
        if 0 <= t - 7 < CHUNKS:
            return_z(t - 7)
        if t == CHUNKS:
            attend_end()
    total = final_own[...]
    for o in PLACE:
        if o:
            k = PLACE[o]
            last_z(o).wait_recv()
            total = total + last_got[k].astype(F32)
    finals[x] = total.astype(BF16)
    for d in (1, 3, 2):
        out_copy(d).start()
    for d in (1, 3, 2):
        out_copy_in(d).wait_recv()
    for i in range(X):
        out_ref[:, i * QUARTER : (i + 1) * QUARTER] = finals[i]

    for d in (1, 2, 3):
        att_copy(d).wait_send()
        att_top_copy(d).wait_send()
        out_copy(d).wait_send()
        for k in range(CHUNKS):
            sums_copy(k, d).wait_send()
            act_copy(k, d).wait_send()
            back_y(k, d).wait_send()
        for o in PLACE:
            fan(o, d).wait_send()
    for o in PLACE:
        if o:
            last_z(o).wait_send()
    spread(4).wait_send()
    for k in range(CHUNKS):
        pass_on(k).wait_send()
        give(k).wait_send()


def shards(query, cache, lengths, blocks, moe_tokens, routes, route_weights, w_gate, w_up, w_down):
    smem = pl.BlockSpec(memory_space=pltpu.SMEM)
    vmem = pl.BlockSpec(memory_space=pltpu.VMEM)
    hbm = pl.BlockSpec(memory_space=pl.ANY)
    scratch = lambda *shape: pltpu.VMEM(shape, BF16)
    wide = lambda *shape: pltpu.VMEM(shape, F32)
    return pl.pallas_call(
        kernel,
        out_shape=(
            jax.ShapeDtypeStruct((2, HEAD_SHARE, KV), BF16),
            jax.ShapeDtypeStruct((ROWS, X * QUARTER), BF16),
        ),
        in_specs=[smem, smem, vmem, vmem] + [hbm] * 6,
        out_specs=(vmem, vmem),
        scratch_shapes=[
            scratch(ROWS, WIDE),
            scratch(CHUNKS, Y, 2, ROWS, WIDE),
            scratch(QUARTER, UNITS),
            scratch(QUARTER, UNITS),
            scratch(UNITS, QUARTER),
            scratch(2, WIDTH, HEADS),
            scratch(2, WIDTH, SPAN),
            wide(X, 2, HEAD_SHARE, KV),
            scratch(X, 2, HEAD_SHARE, KV),
            wide(X, 2, HEAD_SHARE, 128),
            scratch(3, 2, HEAD_SHARE, KV),
            wide(3, 2, HEAD_SHARE, 128),
            scratch(CHUNK_ROWS, CHUNK_ROWS),
            scratch(CHUNKS, CHUNK_ROWS, SLOTS),
            wide(CHUNKS, CHUNK_ROWS, 128),
            wide(CHUNKS, X, SLOTS, 2 * SHARE),
            scratch(CHUNKS, X, SLOTS, 2 * SHARE),
            scratch(CHUNKS, 3, SLOTS, 2 * SHARE),
            scratch(CHUNKS, X, SLOTS, SHARE),
            wide(CHUNKS, Y, 2, ROWS, QUARTER),
            wide(CHUNKS, Y, ROWS, QUARTER),
            wide(CHUNKS, Y, ROWS, QUARTER),
            scratch(CHUNKS, Y, ROWS, QUARTER),
            scratch(CHUNKS, 3, ROWS, QUARTER),
            wide(ROWS, QUARTER),
            scratch(CHUNKS, ROWS, QUARTER),
            scratch(CHUNKS, ROWS, QUARTER),
            scratch(X, ROWS, QUARTER),
            pltpu.SemaphoreType.DMA((7,)),
            pltpu.SemaphoreType.DMA((len(COPIES),)),
            pltpu.SemaphoreType.DMA((len(COPIES),)),
        ],
        compiler_params=pltpu.CompilerParams(
            collective_id=0, has_side_effects=True, vmem_limit_bytes=62 * 1024 * 1024
        ),
    )(
        blocks, lengths, routes.T, route_weights.T, moe_tokens, jnp.swapaxes(query, 1, 2), jnp.swapaxes(cache, 1, 2),
        w_gate, w_up, w_down,
    )


def solution(mesh):
    return jax.shard_map(
        shards,
        mesh=mesh,
        in_specs=(
            P("expert", None, None),
            P("expert", "ctx", None),
            P("expert"),
            P("expert", None),
            P("expert", None),
            P("expert", None),
            P("expert", None),
            P("ctx", "expert"),
            P("ctx", "expert"),
            P("expert", "ctx"),
        ),
        out_specs=(P("expert", "ctx", None), P("expert", None)),
        check_vma=False,
    )
```

time: 362 us -> 77.2 us (0.21)
  waiting for transfers between devices: 167 us -> 0 us
  blocking collectives: 125 us -> 0 us
  Pallas kernels: 0 us -> 72.5 us
  matrix products: 21.3 us -> 0 us
  between operations: 14.3 us -> 0.64 us
  local copies, waits for them, and re-layouts: 15.3 us -> 3.11 us
  starting transfers between devices: 11.1 us -> 0 us
  other arithmetic: 7.89 us -> 0 us
    all_to_all x1 -> x0, blocking collectives: 97 us -> none  [shards(): lax.all_to_all(outgoing, 'expert', split_axis=0, concat_axis=0, tiled=True)]
    psum x1 -> x0, waiting for transfers between devices: 77.4 us -> none  [shards(): gate_sum, up_sum = lax.psum((gate_sum, up_sum), 'ctx')]
    all_to_all x1 -> x0, waiting for transfers between devices: 74.7 us -> none  [shards(): lax.all_to_all(jnp.einsum('sqnf,qfd->sqnd', activated, down_local, prefer...]
    pallas_call x0 -> x1, Pallas kernels: none -> 72.5 us  [shards(): pl.pallas_call(kernel, out_shape=(jax.ShapeDtypeStruct((2, HEAD_SHARE, KV...]
    all_gather x3 -> x0, blocking collectives: 28.1 us -> none  [the longest x2 16 us: joined(): gathered = jax.tree.map(lambda a: lax.all_gather(a, axis), part)]
    dot_general x7 -> x0, matrix products: 21.3 us -> none  [the longest x1 5.09 us: shards(): jnp.einsum('rht,rtc->rhc', weights, latent_values, precision=lax.Precisio...]
    all_gather x1 -> x0, waiting for transfers between devices: 14.7 us -> none  [joined(): gathered = jax.tree.map(lambda a: lax.all_gather(a, axis), part)]
    all_to_all x1 -> x0, starting transfers between devices: 10.9 us -> none  [shards(): lax.all_to_all(jnp.einsum('sqnf,qfd->sqnd', activated, down_local, prefer...]
  transfers between devices with their start and end apart: 3 -> 0, of which waited for: 3 -> 0; matrix products, arithmetic and copies ran while one was open for 5% -> 0% of each run, Pallas kernels for 0% -> 0%
where the time goes in v2:
time: 77.2 us; the launch traced here: 76.2 us
  Pallas kernels  72.5 us (94%)
  local copies, waits for them, and re-layouts  3.11 us (4%)
    pallas_call x1, Pallas kernels, shards(): pl.pallas_call(kernel, out_shape=(jax.ShapeDtypeStruct((2, HEAD_SHARE, KV...  72.5 us
    unnamed x2, local copies, waits for them, and re-layouts  3.11 us

profile of v2, /device:TPU:8, one launch (start us, length us, event | category | flops | bytes accessed | tf_op | source)
XLA Modules:
  0.0 76.2 jit_solution(7377409085573328385)
XLA Ops:
  0.6 72.5 %shard_map.113 = (bf16[2,32,512]{2,1,0:T(8,128)(2,1)}, bf16[16,7168]{1,0:T(8,128)(2,1)}) custom-call(s32[2,32]{1,0:T(2,128)} %blocks_ref.1, s32[2]{0:T(128)} %lengths_ref.1, s32[8,16]{1,0:T(8,128)} %bitcast.6, f32[8,16]{1,0:T(8,128)} %bitcast.7, bf16[16,7168]{1,0:T(8,128)(2,1)} %tokens_hbm.1, bf16[2,576,128]{2,1,0:T(8,128)(2,1)} %bitcast.5, ...), custom_call_target="tpu_custom_call" | custom-call | tf_op jit(solution)/shard_map/pallas_call | solution.py:401
  73.1 1.5 %copy.14 = bf16[2,32,512]{2,1,0:T(8,128)(2,1)} copy(bf16[2,32,512]{2,1,0:T(8,128)(2,1)} %get-tuple-element.4) | data formatting | bytes 131072
  74.6 1.6 %copy.15 = bf16[16,7168]{1,0:T(8,128)(2,1)} copy(bf16[16,7168]{1,0:T(8,128)(2,1)} %get-tuple-element.5) | data formatting | bytes 458752

commit v3 on v2

--- a/solution.py
+++ b/solution.py
@@ -338,7 +338,7 @@
     gather(0)
     loads[4].wait()
     loads[5].wait()
-    for t in range(CHUNKS + 7):
+    for t in range(CHUNKS + 8):
         if t + 3 < CHUNKS:
             fan_out(t + 3)
         if t == 0:
@@ -349,14 +349,14 @@
             chunk(t)
         if t == 3:
             loads[6].wait()
-        if 0 <= t - 2 < CHUNKS:
-            activate(t - 2)
-        if 0 <= t - 4 < CHUNKS:
-            finish(t - 4)
+        if 0 <= t - 3 < CHUNKS:
+            activate(t - 3)
         if 0 <= t - 5 < CHUNKS:
-            return_y(t - 5)
-        if 0 <= t - 7 < CHUNKS:
-            return_z(t - 7)
+            finish(t - 5)
+        if 0 <= t - 6 < CHUNKS:
+            return_y(t - 6)
+        if 0 <= t - 8 < CHUNKS:
+            return_z(t - 8)
         if t == CHUNKS:
             attend_end()
     total = final_own[...]

time: 77.2 us -> 79.4 us (1.028)
  Pallas kernels: 72.5 us -> 74.1 us
    pallas_call x1, Pallas kernels: 72.5 us -> 74.1 us  [shards(): pl.pallas_call(kernel, out_shape=(jax.ShapeDtypeStruct((2, HEAD_SHARE, KV...]
where the time goes in v3:
time: 79.4 us; the launch traced here: 77.9 us
  Pallas kernels  74.1 us (93%)
  local copies, waits for them, and re-layouts  3.11 us (4%)
    pallas_call x1, Pallas kernels, shards(): pl.pallas_call(kernel, out_shape=(jax.ShapeDtypeStruct((2, HEAD_SHARE, KV...  74.1 us
    unnamed x2, local copies, waits for them, and re-layouts  3.11 us

profile of v3, /device:TPU:8, one launch (start us, length us, event | category | flops | bytes accessed | tf_op | source)
XLA Modules:
  0.0 77.9 jit_solution(16008951741097728506)
XLA Ops:
  0.6 74.1 %shard_map.113 = (bf16[2,32,512]{2,1,0:T(8,128)(2,1)}, bf16[16,7168]{1,0:T(8,128)(2,1)}) custom-call(s32[2,32]{1,0:T(2,128)} %blocks_ref.1, s32[2]{0:T(128)} %lengths_ref.1, s32[8,16]{1,0:T(8,128)} %bitcast.6, f32[8,16]{1,0:T(8,128)} %bitcast.7, bf16[16,7168]{1,0:T(8,128)(2,1)} %tokens_hbm.1, bf16[2,576,128]{2,1,0:T(8,128)(2,1)} %bitcast.5, ...), custom_call_target="tpu_custom_call" | custom-call | tf_op jit(solution)/shard_map/pallas_call | solution.py:401
  74.8 1.5 %copy.14 = bf16[2,32,512]{2,1,0:T(8,128)(2,1)} copy(bf16[2,32,512]{2,1,0:T(8,128)(2,1)} %get-tuple-element.4) | data formatting | bytes 131072
  76.2 1.6 %copy.15 = bf16[16,7168]{1,0:T(8,128)(2,1)} copy(bf16[16,7168]{1,0:T(8,128)(2,1)} %get-tuple-element.5) | data formatting | bytes 458752

commit v4 on v2

--- a/solution.py
+++ b/solution.py
@@ -343,22 +343,22 @@
             fan_out(t + 3)
         if t == 0:
             spread_next((3, -3), (4,))
-        if t + 1 < CHUNKS:
-            gather(t + 1)
+        if 0 <= t - 2 < CHUNKS:
+            activate(t - 2)
         if t < CHUNKS:
             chunk(t)
         if t == 3:
             loads[6].wait()
-        if 0 <= t - 2 < CHUNKS:
-            activate(t - 2)
         if 0 <= t - 4 < CHUNKS:
             finish(t - 4)
         if 0 <= t - 5 < CHUNKS:
             return_y(t - 5)
         if 0 <= t - 7 < CHUNKS:
             return_z(t - 7)
-        if t == CHUNKS:
+        if t == 4:
             attend_end()
+        if t + 1 < CHUNKS:
+            gather(t + 1)
     total = final_own[...]
     for o in PLACE:
         if o:

time: 77.2 us -> 79.7 us (1.032)
  Pallas kernels: 72.5 us -> 75.5 us
    pallas_call x1, Pallas kernels: 72.5 us -> 75.5 us  [shards(): pl.pallas_call(kernel, out_shape=(jax.ShapeDtypeStruct((2, HEAD_SHARE, KV...]
where the time goes in v4:
time: 79.7 us; the launch traced here: 79.3 us
  Pallas kernels  75.5 us (95%)
  local copies, waits for them, and re-layouts  3.11 us (4%)
    pallas_call x1, Pallas kernels, shards(): pl.pallas_call(kernel, out_shape=(jax.ShapeDtypeStruct((2, HEAD_SHARE, KV...  75.5 us
    unnamed x2, local copies, waits for them, and re-layouts  3.11 us

profile of v4, /device:TPU:8, one launch (start us, length us, event | category | flops | bytes accessed | tf_op | source)
XLA Modules:
  0.0 79.3 jit_solution(15671271443876486670)
XLA Ops:
  0.6 75.5 %shard_map.113 = (bf16[2,32,512]{2,1,0:T(8,128)(2,1)}, bf16[16,7168]{1,0:T(8,128)(2,1)}) custom-call(s32[2,32]{1,0:T(2,128)} %blocks_ref.1, s32[2]{0:T(128)} %lengths_ref.1, s32[8,16]{1,0:T(8,128)} %bitcast.6, f32[8,16]{1,0:T(8,128)} %bitcast.7, bf16[16,7168]{1,0:T(8,128)(2,1)} %tokens_hbm.1, bf16[2,576,128]{2,1,0:T(8,128)(2,1)} %bitcast.5, ...), custom_call_target="tpu_custom_call" | custom-call | tf_op jit(solution)/shard_map/pallas_call | solution.py:401
  76.2 1.5 %copy.14 = bf16[2,32,512]{2,1,0:T(8,128)(2,1)} copy(bf16[2,32,512]{2,1,0:T(8,128)(2,1)} %get-tuple-element.4) | data formatting | bytes 131072
  77.7 1.6 %copy.15 = bf16[16,7168]{1,0:T(8,128)(2,1)} copy(bf16[16,7168]{1,0:T(8,128)(2,1)} %get-tuple-element.5) | data formatting | bytes 458752
